TPU v7x, 32 devices: a whole 2x2x4 slice. The times are simulated.
32 devices in a mesh: lon: 32 (over z, y, x, core), lat: 1.
Axes of the slice: x: 2, y: 2, z: 4, core: 2. Of those that a mesh axis runs over, the one named last changes fastest.
Arguments:
- fields: bfloat16 [4, 24, 1440, 256], P(None, 'lat', 'lon'), may hold values from -6 to 6
- mix_weight: bfloat16 [256, 256], replicated, may hold values from -0.375 to 0.375
- spectral_weight: float32 [2, 352, 256], P(None, 'lon'), may hold values from -6 to 6
- mode_limit: int32 [24], P('lat'), may hold values from 88 to 352, as said below
- land_mask: int32 [24, 1440], P('lat', 'lon'), may hold values 0 or 1
- forcing: float32 [4, 24, 1440, 128], P(None, 'lat', 'lon'), may hold values from -1440 to 1440
Outputs:
- layer_out: bfloat16 [4, 24, 1440, 256], P(None, 'lat', 'lon')
- residual: float32 [4, 24, 1440, 128], P(None, 'lat', 'lon')
Inputs may be any that keep to these rules, and one draw needn't show every extreme that they name: `mode_limit`: some latitude keeps all 352 wavenumbers.
All inputs are finite; a program needn't handle non-finite values. No bound on the sum of `land_mask` on one device may be relied on, other than what follows from the above.
Results may differ from a plain program's by a relative error of at most 0.0055.
Values may be sent and summed in bfloat16 or wider, within the bound.
A program may use at most 64 MiB of HBM per device.

v0:
```python
import math

import jax
import jax.numpy as jnp
from jax import lax
from jax.sharding import PartitionSpec as P


def extended(block, sides, width, periodic):
    for axis, dim in sides:
        count = lax.axis_size(axis)
        forward = [(i, i + 1) for i in range(count - 1)]
        if periodic:
            forward.append((count - 1, 0))
        backward = [(target, source) for source, target in forward]
        low = lax.ppermute(
            lax.slice_in_dim(block, block.shape[dim] - width, None, axis=dim), axis, forward
        )
        high = lax.ppermute(lax.slice_in_dim(block, 0, width, axis=dim), axis, backward)
        block = jnp.concatenate([low, block, high], axis=dim)
    return block


def build_table(length, wavenumbers):
    order = jnp.arange(wavenumbers, dtype=jnp.int32)[:, None]
    places = jnp.arange(length, dtype=jnp.int32)[None, :]
    angles = (order * places % length).astype(jnp.float32) * (2.0 * math.pi / length)
    return jnp.concatenate([jnp.cos(angles), -jnp.sin(angles)], axis=0).astype(jnp.bfloat16)


def filter_modes(coefficients, weight, limits):
    count = weight.shape[1]
    real_in = coefficients[:, :count]
    imag_in = coefficients[:, count:]
    weight_real = weight[0][None]
    weight_imag = weight[1][None]
    real_out = weight_real * real_in - weight_imag * imag_in
    imag_out = weight_real * imag_in + weight_imag * real_in
    order = jnp.arange(count, dtype=jnp.int32)
    keep_modes = (order[None, :] < limits[:, None]).astype(jnp.float32)
    keep_modes = keep_modes * jnp.where(order == 0, 1.0, 2.0).astype(jnp.float32)[None, :]
    joined = jnp.concatenate(
        [real_out * keep_modes[:, :, None], imag_out * keep_modes[:, :, None]], axis=1
    )
    return joined.astype(jnp.bfloat16)


def per_device(fields, mix_weight, spectral_weight, mode_limit, land_mask, forcing):
    members, lat_dev, lon_dev, channels = fields.shape
    half_width = channels // 2
    lon_count = lax.axis_size("lon")
    nlon_total = lon_dev * lon_count
    nlat_total = lat_dev * lax.axis_size("lat")
    row_count = members * lat_dev
    block_rows = row_count // lon_count
    full_weight = lax.all_gather(spectral_weight, "lon", axis=1, tiled=True)
    wavenumbers = full_weight.shape[1]
    flattened = fields.reshape(row_count, lon_dev, channels)
    mixed = jnp.dot(flattened.reshape(-1, channels), mix_weight, preferred_element_type=jnp.float32)
    mixed = mixed.reshape(fields.shape)
    across = lax.all_to_all(flattened, "lon", split_axis=0, concat_axis=1, tiled=True)
    row_ids = lax.axis_index("lon") * block_rows + jnp.arange(block_rows, dtype=jnp.int32)
    limits = jnp.take(mode_limit, row_ids % lat_dev)
    dft_table = build_table(nlon_total, wavenumbers)
    coefficients = jnp.einsum(
        "kl,rlc->rkc", dft_table, across, preferred_element_type=jnp.float32
    ) * (1.0 / nlon_total)
    filtered = filter_modes(coefficients, full_weight, limits)
    spectral = jnp.einsum(
        "kl,rkc->rlc", dft_table, filtered, preferred_element_type=jnp.float32
    ).astype(jnp.bfloat16)
    slope_scale = nlon_total / (4.0 * math.pi)
    returned = lax.all_to_all(spectral, "lon", split_axis=1, concat_axis=0, tiled=True).reshape(
        fields.shape
    )
    summed = returned.astype(jnp.float32) + mixed
    layer_out = (fields.astype(jnp.float32) + jax.nn.gelu(summed)).astype(jnp.bfloat16)
    padded_zonal = extended(layer_out[..., :half_width], (("lon", 2),), 1, True)
    padded_zonal = padded_zonal.astype(jnp.float32)
    zonal = (padded_zonal[:, :, 2:] - padded_zonal[:, :, :-2]) * slope_scale
    padded_merid = extended(layer_out[..., half_width:], (("lat", 1),), 1, False)
    lat_ids = lax.axis_index("lat") * lat_dev + jnp.arange(-1, lat_dev + 1, dtype=jnp.int32)
    latitude = -0.5 * math.pi + (lat_ids.astype(jnp.float32) + 0.5) * (math.pi / nlat_total)
    cos_lat = jnp.cos(latitude)
    weighted = padded_merid.astype(jnp.float32) * cos_lat[None, :, None, None]
    meridional = (weighted[:, 2:] - weighted[:, :-2]) * (nlat_total / (2.0 * math.pi))
    ocean = land_mask.astype(jnp.float32)[None, :, :, None]
    raw = ocean * (zonal + meridional + cos_lat[1:-1][None, :, None, None] * forcing)
    total = lax.psum(jnp.sum(raw * raw), ("lon", "lat"))
    norm = jnp.sqrt(total / (members * nlat_total * nlon_total * half_width) + 1e-06)
    return (layer_out, raw / norm)


def solution(mesh):
    placed = (
        P(None, "lat", "lon", None),
        P(),
        P(None, "lon", None),
        P("lat"),
        P("lat", "lon"),
        P(None, "lat", "lon", None),
    )
    return jax.shard_map(
        per_device,
        mesh=mesh,
        in_specs=placed,
        out_specs=(P(None, "lat", "lon", None), P(None, "lat", "lon", None)),
        check_vma=False,
    )
```

profile of v0, /device:TPU:0, one launch (start us, length us, event | category | flops | bytes accessed | tf_op | source)
XLA Modules:
  0.0 266.1 jit_solution(16597624959822859855)
XLA Ops:
  0.6 1.9 copy.39
  2.6 2.7 %copy.40 = bf16[96,45,256]{2,1,0:T(8,128)(2,1)} copy(bf16[96,45,256]{2,0,1:T(8,128)(2,1)S(1)} %bitcast.32) | data formatting | bytes 4423680 | tf_op jit(solution)/shard_map/reshape | solution.py:58
  5.3 7.3 %all-to-all-start = ((bf16[96,45,256]{2,1,0:T(8,128)(2,1)}), bf16[96,45,256]{2,1,0:T(8,128)(2,1)S(1)}, u32[]{:S(2)}, u32[]{:S(2)}) async-start(bf16[96,45,256]{2,1,0:T(8,128)(2,1)} %copy.40), calls=%async_computation | async-start | bytes 4718592 | tf_op jit(solution)/shard_map/all_to_all | solution.py:61
  12.7 0.6 gather_fusion
  13.4 76.3 %all_gather.3 = f32[2,352,256]{2,0,1:T(2,128)S(1)} all-gather(f32[2,11,256]{2,0,1:T(2,128)S(1)} %copy-done.6), channel_id=1, replica_groups=mesh['lon'=32,'lat'=1] {'lon'}, dimensions={1}, use_global_device_ids=true | all-gather | bytes 743424 | tf_op jit(solution)/shard_map/all_gather | solution.py:56
  89.7 0.6 fusion.34
  90.3 10.4 %negate_convert_fusion = (bf16[352,1440]{1,0:T(8,128)(2,1)}, bf16[352,1440]{1,0:T(8,128)(2,1)}) fusion(), kind=kLoop, calls=%fused_computation.31 | loop fusion | flops 6082560 | bytes 2027520 | tf_op jit(solution)/shard_map/convert.6
  100.7 1.6 copy.41
  102.4 2.7 %all_to_all.23 = bf16[3,1440,256]{2,1,0:T(8,128)(2,1)S(1)} reshape(bf16[3,32,45,256]{3,2,1,0:T(8,128)(2,1)} %copy.41) | data formatting | bytes 4423680 | tf_op jit(solution)/shard_map/all_to_all | solution.py:61
  105.1 3.4 %multiply_bitcast_fusion = f32[3,704,256]{2,1,0:T(8,128)S(1)} fusion(bf16[3,1440,256]{2,1,0:T(8,128)(2,1)S(1)} %all_to_all.23, bf16[352,1440]{1,0:T(8,128)(2,1)} %get-tuple-element.22, bf16[352,1440]{1,0:T(8,128)(2,1)} %get-tuple-element.23), kind=kOutput, calls=%fused_computation.30 | convolution fusion | flops 1561731072 | bytes 6402048 | tf_op jit(solution)/shard_map/kl,rlc->rkc/dot_general | solution.py:65
  108.5 0.4 multiply_convert_fusion.1
  108.9 0.8 copy-done.4
  109.8 0.3 copy-done.5
  110.1 1.9 fusion.9
  112.0 12.3 %copy.43 = bf16[3,1440,256]{2,0,1:T(4,128)(2,1)} copy(bf16[3,1440,256]{2,1,0:T(8,128)(2,1)S(1)} %fusion.9) | data formatting | bytes 4423680 | tf_op jit(solution)/shard_map/convert_element_type | solution.py:71
  124.4 7.7 %all-to-all-start.1 = ((bf16[3,1440,256]{2,0,1:T(4,128)(2,1)}), bf16[3,1440,256]{2,0,1:T(4,128)(2,1)S(1)}, u32[]{:S(2)}, u32[]{:S(2)}) async-start(bf16[3,1440,256]{2,0,1:T(4,128)(2,1)} %copy.43), calls=%async_computation.1 | async-start | bytes 5898240 | tf_op jit(solution)/shard_map/all_to_all | solution.py:73
  132.2 67.0 %all-to-all-done.1 = bf16[3,1440,256]{2,0,1:T(4,128)(2,1)S(1)} async-done(((bf16[3,1440,256]{2,0,1:T(4,128)(2,1)}), bf16[3,1440,256]{2,0,1:T(4,128)(2,1)S(1)}, u32[]{:S(2)}, u32[]{:S(2)}) %all-to-all-start.1) | async-done | bytes 2211872 | tf_op jit(solution)/shard_map/all_to_all | solution.py:73
  199.2 2.5 copy_convert_fusion
  201.7 5.0 %reshape.114 = f32[3,32,45,256]{3,2,1,0:T(8,128)} reshape(f32[3,1440,256]{2,1,0:T(8,128)} %copy_convert_fusion) | data formatting | bytes 8847360 | tf_op jit(solution)/shard_map/convert_element_type | solution.py:76
  206.7 2.8 %copy.45 = f32[32,3,45,256]{3,2,1,0:T(8,128)S(1)} copy(f32[32,3,45,256]{3,2,0,1:T(8,128)} %bitcast.30) | data formatting | bytes 8847360 | tf_op jit(solution)/shard_map/convert_element_type | solution.py:76
  209.7 2.6 fusion.8
  212.5 0.4 fusion.32
  213.0 5.3 %collective-permute-start.1 = (bf16[4,24,1,128]{3,2,1,0:T(2,128)(2,1)S(1)}, bf16[4,24,1,128]{3,2,1,0:T(2,128)(2,1)S(1)}, u32[]{:S(2)}, u32[]{:S(2)}) collective-permute-start(bf16[4,24,1,128]{3,2,1,0:T(2,128)(2,1)S(1)} %get-tuple-element.15), channel_id=1, source_target_pairs={{1,0},{2,1},{3,2},{4,3},{5,4},{6,5},{7,6},{8,7},{9,8},{10,9},{11,1... | collective-permute-start | bytes 73736 | tf_op jit(solution)/shard_map/ppermute | solution.py:19
  218.3 2.2 copy.48
  220.5 0.6 collective-permute-start.2
  221.1 0.7 collective-permute-start.3
  221.8 0.5 maximum_convert_fusion
  222.3 0.3 convert_multiply_fusion
  222.7 1.3 copy-done.3
  223.9 2.2 multiply_reduce_fusion
  226.1 37.1 %psum.7 = f32[]{:T(128)} all-reduce(f32[]{:T(128)} %get-tuple-element.10), channel_id=1, replica_groups=mesh['lon'=32,'lat'=1] {'lon','lat'}, use_global_device_ids=true, to_apply=%region_1.2 | all-reduce | flops 1 | bytes 8 | tf_op jit(solution)/shard_map/psum | solution.py:89
  264.1 2.0 copy.49
  (31 shorter events, 0.9 us)
Async XLA Ops:
  0.6 208.9 %copy-start = (bf16[256,256]{1,0:T(8,128)(2,1)S(1)}, bf16[256,256]{1,0:T(8,128)(2,1)}, u32[]{:S(2)}) copy-start(bf16[256,256]{1,0:T(8,128)(2,1)} %param.7) | copy-start | bytes 393220
  5.3 7.3 %copy-start.1 = (s32[24]{0:T(128)S(1)}, s32[24]{0:T(128)}, u32[]{:S(2)}) copy-start(s32[24]{0:T(128)} %param.9) | copy-start | bytes 292
  5.3 8.1 %copy-start.6 = (f32[2,11,256]{2,0,1:T(2,128)S(1)}, f32[2,11,256]{2,0,1:T(2,128)}, u32[]{:S(2)}) copy-start(f32[2,11,256]{2,0,1:T(2,128)} %param.8) | copy-start | bytes 67588
  5.3 95.4 %all-to-all-start = ((bf16[96,45,256]{2,1,0:T(8,128)(2,1)}), bf16[96,45,256]{2,1,0:T(8,128)(2,1)S(1)}, u32[]{:S(2)}, u32[]{:S(2)}) async-start(bf16[96,45,256]{2,1,0:T(8,128)(2,1)} %copy.40), calls=%async_computation | async-start | bytes 4718592 | tf_op jit(solution)/shard_map/all_to_all | solution.py:61
  108.5 1.2 copy-start.4
  108.5 1.6 copy-start.5
  124.4 7.9 %copy-start.7 = (s32[24,45]{1,0:T(8,128)S(1)}, s32[24,45]{1,0:T(8,128)}, u32[]{:S(2)}) copy-start(s32[24,45]{1,0:T(8,128)} %param.10) | copy-start | bytes 12964
  124.4 74.8 %all-to-all-start.1 = ((bf16[3,1440,256]{2,0,1:T(4,128)(2,1)}), bf16[3,1440,256]{2,0,1:T(4,128)(2,1)S(1)}, u32[]{:S(2)}, u32[]{:S(2)}) async-start(bf16[3,1440,256]{2,0,1:T(4,128)(2,1)} %copy.43), calls=%async_computation.1 | async-start | bytes 5898240 | tf_op jit(solution)/shard_map/all_to_all | solution.py:73
  206.7 3.0 %copy-start.2 = (bf16[4,24,45,256]{3,1,2,0:T(8,128)(2,1)S(1)}, bf16[4,24,45,256]{3,1,2,0:T(8,128)(2,1)}, u32[]{:S(2)}) copy-start(bf16[4,24,45,256]{3,1,2,0:T(8,128)(2,1)} %param.6) | copy-start | bytes 6635524
  212.9 8.9 %collective-permute-start = (bf16[4,24,1,128]{3,2,1,0:T(2,128)(2,1)S(1)}, bf16[4,24,1,128]{3,2,1,0:T(2,128)(2,1)S(1)}, u32[]{:S(2)}, u32[]{:S(2)}) collective-permute-start(bf16[4,24,1,128]{3,2,1,0:T(2,128)(2,1)S(1)} %get-tuple-element.14), channel_id=1, source_target_pairs={{0,1},{1,2},{2,3},{3,4},{4,5},{5,6},{6,7},{7,8},{8,9},{9,10},{10,1... | collective-permute-start | bytes 73736 | tf_op jit(solution)/shard_map/ppermute | solution.py:16
  213.0 8.8 %collective-permute-start.1 = (bf16[4,24,1,128]{3,2,1,0:T(2,128)(2,1)S(1)}, bf16[4,24,1,128]{3,2,1,0:T(2,128)(2,1)S(1)}, u32[]{:S(2)}, u32[]{:S(2)}) collective-permute-start(bf16[4,24,1,128]{3,2,1,0:T(2,128)(2,1)S(1)} %get-tuple-element.15), channel_id=1, source_target_pairs={{1,0},{2,1},{3,2},{4,3},{5,4},{6,5},{7,6},{8,7},{9,8},{10,9},{11,1... | collective-permute-start | bytes 73736 | tf_op jit(solution)/shard_map/ppermute | solution.py:19
  220.5 1.8 collective-permute-start.2
  221.1 1.2 collective-permute-start.3
  222.3 1.6 copy-start.3
where the time goes:
time: 268 us; the launch traced here: 266 us
  blocking collectives  113 us (42%)
  waiting for transfers between devices  67 us (25%)
  local copies, waits for them, and re-layouts  37.9 us (14%)
  starting transfers between devices  21.7 us (8%)
  other arithmetic  16.6 us (6%)
  matrix products  7.96 us (3%)
    all_gather x1, blocking collectives, per_device(): full_weight = lax.all_gather(spectral_weight, 'lon', axis=1, tiled=True)  76.3 us
    all_to_all x1, waiting for transfers between devices, per_device(): lax.all_to_all(spectral, 'lon', split_axis=1, concat_axis=0, tiled=True)  67 us
    psum x1, blocking collectives, per_device(): total = lax.psum(jnp.sum(raw * raw), ('lon', 'lat'))  37.1 us
    convert_element_type x1, local copies, waits for them, and re-layouts, per_device(): spectral = jnp.einsum('kl,rkc->rlc', dft_table, filtered, preferred_eleme...  12.3 us
    another operation x2, other arithmetic  10.8 us
    unnamed x19, local copies, waits for them, and re-layouts  8.8 us
    convert_element_type x2, local copies, waits for them, and re-layouts, per_device(): summed = returned.astype(jnp.float32) + mixed  7.85 us
    all_to_all x1, starting transfers between devices, per_device(): lax.all_to_all(spectral, 'lon', split_axis=1, concat_axis=0, tiled=True)  7.72 us
  transfers between devices with their start and end apart: 6, of which 1 were waited for; matrix products, arithmetic and copies ran while one was open for 5% of the time, Pallas kernels for 0%

commit v1 on v0

v1 whole, which is shorter than its diff:
```python
import functools
import math

import jax
import jax.numpy as jnp
import numpy as np
from jax import lax
from jax.experimental import pallas as pl
from jax.experimental.pallas import tpu as pltpu
from jax.sharding import PartitionSpec as P

MESH = pl.DeviceIdType.MESH
PLANE = 8


def tables(length, wavenumbers, count, pad):
    own = length // count
    places = np.arange(count)[:, None] * own + np.arange(pad)[None, :]
    places[:, pad - 1] = np.arange(count) * own - 1
    places = places % length
    order = np.arange(wavenumbers)[:, None, None]
    angles = (order * places[None] % length).astype(np.float32) * np.float32(
        2.0 * math.pi / length
    )
    full = np.concatenate([np.cos(angles), -np.sin(angles)], axis=0)
    inverse = full.reshape(2 * wavenumbers, count * pad).T.astype(jnp.bfloat16)
    full[:, :, own:] = 0.0
    forward = full.reshape(2 * wavenumbers, count * pad)
    return forward.astype(jnp.bfloat16), inverse


def layer_kernel(
    n, lat_dev, own, length, slope, polar, fused,
    fields, mix, weight, limits, table_f, table_i, *rest,
):
    if fused:
        forcing, ocean, cosines, lo, raw, norm = rest[:6]
        rest = rest[6:]
    else:
        lo = rest[0]
        rest = rest[1:]
    (gathered, wr, wi, arrived, filt, outgoing, tf, ti, force, sums,
     fwd_send, fwd_recv, ret_send, ret_recv, gat_send, gat_recv,
     local_sem, sum_send, sum_recv) = rest
    rows, pad, channels = fields.shape
    chunks = rows // n
    per = weight.shape[1]
    modes = per * n
    me = lax.axis_index("lon")
    groups = n // PLANE
    mine = lax.rem(me, PLANE)
    plane = me // PLANE
    stride = n // 3 + 1
    while math.gcd(stride, n) > 1:
        stride += 1

    def send(src, dst, s_sem, r_sem, to):
        return pltpu.make_async_remote_copy(
            src_ref=src, dst_ref=dst, send_sem=s_sem, recv_sem=r_sem,
            device_id={"lon": to}, device_id_type=MESH,
        )

    def await_bytes(ref, sem):
        pltpu.make_async_copy(ref, ref, sem).wait()

    barrier = pltpu.get_barrier_semaphore()

    @pl.loop(1, n)
    def _(i):
        pl.semaphore_signal(
            barrier, inc=1, device_id={"lon": lax.rem(me + i, n)}, device_id_type=MESH
        )

    loads = [
        pltpu.make_async_copy(table_f, tf, local_sem.at[0]),
        pltpu.make_async_copy(table_i, ti, local_sem.at[1]),
    ]
    if fused:
        loads.append(pltpu.make_async_copy(forcing, force, local_sem.at[2]))
    for load in loads:
        load.start()

    slot = mine * groups + plane
    gathered[slot, 0:per] = weight[0]
    gathered[slot, per:2 * per] = weight[1]

    @pl.loop(0, chunks)
    def _(c):
        place = pl.multiple_of(me * pad, 16)
        arrived[c, pl.ds(place, pad)] = fields[c * n + me]

    pl.semaphore_wait(barrier, n - 1)

    @pl.loop(1, groups)
    def _(i):
        to = lax.rem(plane + i, groups) * PLANE + mine
        send(gathered.at[slot], gathered.at[slot], gat_send.at[0], gat_recv.at[0], to).start()

    def scatter(c):
        @pl.loop(1, n)
        def _(i):
            to = lax.rem(me + lax.rem(i * stride, n), n)
            place = pl.multiple_of(me * pad, 16)
            send(
                fields.at[c * n + to], arrived.at[c, pl.ds(place, pad)],
                fwd_send, fwd_recv.at[c], to,
            ).start()

    scatter(0)
    if groups > 1:
        await_bytes(gathered.at[pl.ds(0, groups - 1)], gat_recv.at[0])
    held = gathered.at[pl.ds(mine * groups, groups)]

    @pl.loop(1, PLANE)
    def _(i):
        to = plane * PLANE + lax.rem(mine + i, PLANE)
        send(held, held, gat_send.at[1], gat_recv.at[1], to).start()

    for c in range(1, chunks):
        scatter(c)

    await_bytes(gathered.at[pl.ds(0, n - groups)], gat_recv.at[1])
    for device in range(n):
        place = (device % PLANE) * groups + device // PLANE
        wr[device * per:(device + 1) * per] = gathered[place, 0:per]
        wi[device * per:(device + 1) * per] = gathered[place, per:2 * per]
    loads[0].wait()
    loads[1].wait()

    @pl.loop(0, chunks)
    def _(c):
        await_bytes(arrived.at[c, pl.ds(0, (n - 1) * pad)], fwd_recv.at[c])
        tail = pad - 16
        spot = lax.broadcasted_iota(jnp.int32, (16, channels), 0)

        @pl.loop(0, n)
        def _(d):
            after = pl.multiple_of(lax.rem(d + 1, n) * pad, 16)
            before = pl.multiple_of(lax.rem(d + n - 1, n) * pad + tail, 16)
            here = pl.ds(pl.multiple_of(d * pad + tail, 16), 16)
            first = arrived[c, pl.ds(after, 16)].astype(jnp.float32)
            last = arrived[c, pl.ds(before, 16)].astype(jnp.float32)
            block = arrived[c, here].astype(jnp.float32)
            block = jnp.where(spot == own - tail, pltpu.roll(first, own - tail, 0), block)
            block = jnp.where(spot == 15, pltpu.roll(last, pad - own, 0), block)
            arrived[c, here] = block.astype(jnp.bfloat16)

        whole = arrived[c]
        real = jnp.dot(tf[0:modes], whole, preferred_element_type=jnp.float32) * (1.0 / length)
        imag = jnp.dot(tf[modes:], whole, preferred_element_type=jnp.float32) * (1.0 / length)
        limit = limits[lax.rem(c * n + me, lat_dev)]
        order = lax.broadcasted_iota(jnp.int32, (modes, channels), 0)
        keep = jnp.where(order < limit, jnp.where(order == 0, 1.0, 2.0), 0.0)
        filt[0:modes] = ((wr[...] * real - wi[...] * imag) * keep).astype(jnp.bfloat16)
        filt[modes:] = ((wr[...] * imag + wi[...] * real) * keep).astype(jnp.bfloat16)
        size = PLANE * pad

        @pl.loop(0, groups)
        def _(t):
            target = lax.rem(plane + groups // 2 + t * (groups - 1), groups)
            part = pl.ds(pl.multiple_of(target * size, 16), size)
            here = arrived[c, part]
            spectral = jnp.dot(ti[part], filt[...], preferred_element_type=jnp.float32)
            mixed = jnp.dot(here, mix[...], preferred_element_type=jnp.float32)
            summed = spectral.astype(jnp.bfloat16).astype(jnp.float32) + mixed
            done = here.astype(jnp.float32) + jax.nn.gelu(summed, approximate=True)
            outgoing[pl.ds(c * n + target * PLANE, PLANE)] = done.astype(
                jnp.bfloat16
            ).reshape(PLANE, pad, channels)

            @pl.loop(0, PLANE)
            def _(q):
                to = target * PLANE + lax.rem(mine + q, PLANE)

                @pl.when(to != me)
                def _():
                    send(
                        outgoing.at[c * n + to], lo.at[c * n + me],
                        ret_send, ret_recv.at[c * n + me], to,
                    ).start()

        lo[c * n + me] = outgoing[c * n + me]

    def await_row(r):
        @pl.when(lax.rem(r, n) != me)
        def _():
            await_bytes(lo.at[r], ret_recv.at[r])

    if fused:
        loads[2].wait()
        half = channels // 2
        sums[me] = jnp.zeros((8, half), jnp.float32)

        def residual(r):
            j = lax.rem(r, lat_dev)
            zonal = lo[r, :, 0:half].astype(jnp.float32)
            zonal = (pltpu.roll(zonal, pad - 1, 0) - pltpu.roll(zonal, 1, 0)) * slope
            north = lo[jnp.minimum(r + 1, rows - 1), :, half:].astype(jnp.float32)
            south = lo[jnp.maximum(r - 1, 0), :, half:].astype(jnp.float32)
            merid = (north * cosines[j + 2] - south * cosines[j]) * polar
            flow = (zonal + merid)[0:own]
            value = ocean[j] * (flow + cosines[j + 1] * force[r])
            raw[r] = value
            sums[me, 0:1] += jnp.sum(value * value, axis=0, keepdims=True)

        await_row(0)

        @pl.loop(1, rows)
        def _(r):
            await_row(r)
            residual(r - 1)

        residual(rows - 1)

        @pl.loop(1, n)
        def _(i):
            to = lax.rem(me + i, n)
            send(sums.at[me], sums.at[me], sum_send, sum_recv, to).start()

        await_bytes(sums.at[pl.ds(0, n - 1)], sum_recv)
        total = jnp.sum(sums[...], axis=0)
        total = jnp.sum(jnp.sum(total, axis=0, keepdims=True), axis=1, keepdims=True)
        scale = 1.0 / (rows * own * n * half)
        norm[...] = jnp.broadcast_to(jnp.sqrt(total * scale + 1e-06), (8, half))
        await_bytes(sums.at[pl.ds(0, n - 1)], sum_send)
    else:
        @pl.loop(0, rows)
        def _(r):
            await_row(r)

    await_bytes(fields.at[pl.ds(0, chunks * (n - 1))], fwd_send)
    await_bytes(outgoing.at[pl.ds(0, chunks * (n - 1))], ret_send)
    if groups > 1:
        await_bytes(gathered.at[pl.ds(0, groups - 1)], gat_send.at[0])
    await_bytes(gathered.at[pl.ds(0, (PLANE - 1) * groups)], gat_send.at[1])


def extended(block, axis, dim):
    count = lax.axis_size(axis)
    forward = [(i, i + 1) for i in range(count - 1)]
    if axis == "lon":
        forward.append((count - 1, 0))
    backward = [(target, source) for source, target in forward]
    low = lax.ppermute(lax.slice_in_dim(block, block.shape[dim] - 1, None, axis=dim), axis, forward)
    high = lax.ppermute(lax.slice_in_dim(block, 0, 1, axis=dim), axis, backward)
    return jnp.concatenate([low, block, high], axis=dim)


def per_device(fields, mix_weight, spectral_weight, mode_limit, land_mask, forcing):
    members, lat_dev, own, channels = fields.shape
    half = channels // 2
    n = lax.axis_size("lon")
    lat_count = lax.axis_size("lat")
    length = own * n
    nlat = lat_dev * lat_count
    rows = members * lat_dev
    chunks = rows // n
    per = spectral_weight.shape[1]
    modes = per * n
    pad = -(-(own + 2) // 16) * 16
    fused = lat_count == 1
    forward, inverse = tables(length, modes, n, pad)
    slope = length / (4.0 * math.pi)
    polar = nlat / (2.0 * math.pi)
    padded = jnp.pad(fields.reshape(rows, own, channels), ((0, 0), (0, pad - own), (0, 0)))
    vmem = pl.BlockSpec(memory_space=pltpu.VMEM)
    smem = pl.BlockSpec(memory_space=pltpu.SMEM)
    away = pl.BlockSpec(memory_space=pl.ANY)
    operands = [padded, mix_weight, spectral_weight, mode_limit,
                jnp.asarray(forward), jnp.asarray(inverse)]
    in_specs = [vmem, vmem, vmem, smem, away, away]
    out_shape = [jax.ShapeDtypeStruct((rows, pad, channels), jnp.bfloat16)]
    if fused:
        latitude = np.float32(-0.5 * math.pi) + (
            np.arange(nlat, dtype=np.float32) + np.float32(0.5)
        ) * np.float32(math.pi / nlat)
        cosines = np.zeros((nlat + 2,), np.float32)
        cosines[1:-1] = np.cos(latitude)
        ocean = jnp.broadcast_to(
            land_mask.astype(jnp.float32)[:, :, None], (lat_dev, own, half)
        )
        operands += [forcing.reshape(rows, own, half), ocean, jnp.asarray(cosines)]
        in_specs += [away, vmem, smem]
        out_shape += [
            jax.ShapeDtypeStruct((rows, own, half), jnp.float32),
            jax.ShapeDtypeStruct((8, half), jnp.float32),
        ]
    gat_rows = -(-2 * per // 8) * 8
    dma = pltpu.SemaphoreType.DMA
    results = pl.pallas_call(
        functools.partial(
            layer_kernel, n, lat_dev, own, length, slope, polar, fused
        ),
        out_shape=out_shape,
        in_specs=in_specs,
        out_specs=[vmem] * len(out_shape),
        scratch_shapes=[
            pltpu.VMEM((n, gat_rows, channels), jnp.float32),
            pltpu.VMEM((modes, channels), jnp.float32),
            pltpu.VMEM((modes, channels), jnp.float32),
            pltpu.VMEM((chunks, n * pad, channels), jnp.bfloat16),
            pltpu.VMEM((2 * modes, channels), jnp.bfloat16),
            pltpu.VMEM((rows, pad, channels), jnp.bfloat16),
            pltpu.VMEM(forward.shape, jnp.bfloat16),
            pltpu.VMEM(inverse.shape, jnp.bfloat16),
            pltpu.VMEM((rows, own, half) if fused else (8, half), jnp.float32),
            pltpu.VMEM((n, 8, half), jnp.float32),
            dma, dma((chunks,)), dma, dma((rows,)), dma((2,)), dma((2,)),
            dma((3,)), dma, dma,
        ],
        compiler_params=pltpu.CompilerParams(
            collective_id=0, has_side_effects=True, vmem_limit_bytes=48 * 2**20
        ),
    )(*operands)
    layer_out = results[0][:, :own].reshape(fields.shape)
    if fused:
        residual = results[1].reshape(forcing.shape) / results[2][0]
        return layer_out, residual
    zonal = extended(layer_out[..., :half], "lon", 2).astype(jnp.float32)
    zonal = (zonal[:, :, 2:] - zonal[:, :, :-2]) * slope
    merid = extended(layer_out[..., half:], "lat", 1).astype(jnp.float32)
    lat_ids = lax.axis_index("lat") * lat_dev + jnp.arange(-1, lat_dev + 1, dtype=jnp.int32)
    latitude = -0.5 * math.pi + (lat_ids.astype(jnp.float32) + 0.5) * (math.pi / nlat)
    cos_lat = jnp.cos(latitude)
    weighted = merid * cos_lat[None, :, None, None]
    merid = (weighted[:, 2:] - weighted[:, :-2]) * polar
    ocean = land_mask.astype(jnp.float32)[None, :, :, None]
    raw = ocean * (zonal + merid + cos_lat[1:-1][None, :, None, None] * forcing)
    total = lax.psum(jnp.sum(raw * raw), ("lon", "lat"))
    norm = jnp.sqrt(total / (members * nlat * length * half) + 1e-06)
    return layer_out, raw / norm


def solution(mesh):
    placed = (
        P(None, "lat", "lon", None),
        P(),
        P(None, "lon", None),
        P("lat"),
        P("lat", "lon"),
        P(None, "lat", "lon", None),
    )
    return jax.shard_map(
        per_device,
        mesh=mesh,
        in_specs=placed,
        out_specs=(P(None, "lat", "lon", None), P(None, "lat", "lon", None)),
        check_vma=False,
    )
```

time: 268 us -> 137 us (0.51)
  Pallas kernels: 0 us -> 123 us
  blocking collectives: 113 us -> 0 us
  waiting for transfers between devices: 67 us -> 0 us
  local copies, waits for them, and re-layouts: 37.9 us -> 9.82 us
  starting transfers between devices: 21.7 us -> 0 us
  other arithmetic: 16.6 us -> 2.74 us
  matrix products: 7.96 us -> 0 us
    pallas_call x0 -> x1, Pallas kernels: none -> 123 us  [per_device(): pl.pallas_call(functools.partial(layer_kernel, n, lat_dev, own, length, s...]
    all_gather x1 -> x0, blocking collectives: 76.3 us -> none  [per_device(): full_weight = lax.all_gather(spectral_weight, 'lon', axis=1, tiled=True)]
    all_to_all x2 -> x0, waiting for transfers between devices: 67 us -> none  [the longest x1 67 us: per_device(): lax.all_to_all(spectral, 'lon', split_axis=1, concat_axis=0, tiled=True)]
    psum x1 -> x0, blocking collectives: 37.1 us -> none  [per_device(): total = lax.psum(jnp.sum(raw * raw), ('lon', 'lat'))]
    convert_element_type x3 -> x0, local copies, waits for them, and re-layouts: 20.2 us -> none  [the longest x1 12.3 us: per_device(): spectral = jnp.einsum('kl,rkc->rlc', dft_table, filtered, preferred_eleme...]
    all_to_all x2 -> x0, starting transfers between devices: 15 us -> none  [the longest x1 7.72 us: per_device(): lax.all_to_all(spectral, 'lon', split_axis=1, concat_axis=0, tiled=True)]
    another operation x2 -> x0, other arithmetic: 10.8 us -> none
    dot_general x3 -> x0, matrix products: 7.96 us -> none  [the longest x1 3.4 us: per_device(): jnp.einsum('kl,rlc->rkc', dft_table, across, preferred_element_type=jnp.f...]
  transfers between devices with their start and end apart: 6 -> 0, of which waited for: 1 -> 0; matrix products, arithmetic and copies ran while one was open for 5% -> 0% of each run, Pallas kernels for 0% -> 0%
where the time goes in v1:
time: 137 us; the launch traced here: 136 us
  Pallas kernels  123 us (90%)
  local copies, waits for them, and re-layouts  9.82 us (7%)
  other arithmetic  2.74 us (2%)
    pallas_call x1, Pallas kernels, per_device(): pl.pallas_call(functools.partial(layer_kernel, n, lat_dev, own, length, s...  123 us
    unnamed x16, local copies, waits for them, and re-layouts  8.01 us

profile of v1, /device:TPU:0, one launch (start us, length us, event | category | flops | bytes accessed | tf_op | source)
XLA Modules:
  0.0 136.4 jit_solution(12784804961512342061)
XLA Ops:
  0.6 0.7 convert_element_type.5
  1.3 0.7 copy.13.weight
  2.1 0.2 broadcast_in_dim.2.rest_1_
  2.3 2.1 %copy.11 = bf16[4,24,45,256]{3,2,1,0:T(8,128)(2,1)S(1)} copy(bf16[4,24,45,256]{3,1,2,0:T(8,128)(2,1)} %param.9) | data formatting | bytes 4423680 | tf_op args[0]
  4.4 0.0 copy-start.5
  4.4 1.6 %pad.4.fields = bf16[96,48,256]{2,1,0:T(8,128)(2,1)} pad(bf16[96,45,256]{2,1,0:T(8,128)(2,1)S(1)} %bitcast.9, bf16[]{:T(256)} %constant.8.clone.1), padding=0_0x0_3x0_0 | pad | bytes 4571138 | tf_op jit(solution)/shard_map/jit(_pad)/pad | solution.py:265
  6.0 0.9 copy-done.5
  6.9 0.0 copy-start
  6.9 0.0 copy-start.1
  6.9 0.0 copy-start.2
  6.9 0.0 copy-start.3
  6.9 1.8 %copy.12 = f32[4,24,45,128]{3,2,1,0:T(8,128)} copy(f32[4,24,45,128]{3,1,2,0:T(8,128)S(1)} %copy-done.5) | data formatting | bytes 4423680 | tf_op args[5]
  8.7 0.3 copy-done
  9.0 0.0 copy-done.1
  9.0 0.0 copy-done.2
  9.0 0.0 copy-done.3
  9.0 123.2 %shard_map.104 = (bf16[96,48,256]{2,1,0:T(8,128)(2,1)S(1)}, f32[96,45,128]{2,1,0:T(8,128)}, f32[8,128]{1,0:T(8,128)S(1)}) custom-call(bf16[96,48,256]{2,1,0:T(8,128)(2,1)} %pad.4.fields, bf16[256,256]{1,0:T(8,128)(2,1)S(1)} %copy-done.1, f32[2,11,256]{2,1,0:T(8,128)S(1)} %copy.13.weight, s32[24]{0:T(128)S(1)} %copy-done.2, bf16[704,1536]{1,0:T(8,128)(2,1)S(1)} %copy-done, ...), custom_call_target="tpu_custom_call" | custom-call | tf_op jit(solution)/shard_map/pallas_call | solution.py:290
  132.2 0.0 copy-start.4
  132.2 2.2 %copy.15 = bf16[4,24,45,256]{3,1,2,0:T(8,128)(2,1)} copy(bf16[4,24,45,256]{3,2,1,0:T(8,128)(2,1)S(1)} %bitcast.7) | data formatting | bytes 4423680
  134.4 0.0 copy-done.4
  134.4 2.0 %copy_divide_fusion = f32[4,24,45,128]{3,1,2,0:T(8,128)} fusion(f32[4,24,45,128]{3,2,1,0:T(8,128)S(1)} %bitcast.10, f32[128]{0:T(128)S(1)} %slice_bitcast_fusion), kind=kLoop, calls=%fused_computation | loop fusion | flops 552960 | bytes 4424192 | tf_op jit(solution)/shard_map/div | solution.py:317
  (1 shorter events, 0.0 us)
Async XLA Ops:
  4.4 2.5 %copy-start.5 = (f32[4,24,45,128]{3,1,2,0:T(8,128)S(1)}, f32[4,24,45,128]{3,1,2,0:T(8,128)}, u32[]{:S(2)}) copy-start(f32[4,24,45,128]{3,1,2,0:T(8,128)} %param.14) | copy-start | bytes 6635524
  6.9 2.1 %copy-start = (bf16[704,1536]{1,0:T(8,128)(2,1)S(1)}, bf16[704,1536]{1,0:T(8,128)(2,1)}, u32[]{:S(2)}) copy-start(bf16[704,1536]{1,0:T(8,128)(2,1)} %constant.9.clone.table_f) | copy-start | bytes 6488068
  6.9 2.1 %copy-start.1 = (bf16[256,256]{1,0:T(8,128)(2,1)S(1)}, bf16[256,256]{1,0:T(8,128)(2,1)}, u32[]{:S(2)}) copy-start(bf16[256,256]{1,0:T(8,128)(2,1)} %mix.1) | copy-start | bytes 393220
  6.9 2.1 %copy-start.2 = (s32[24]{0:T(128)S(1)}, s32[24]{0:T(128)}, u32[]{:S(2)}) copy-start(s32[24]{0:T(128)} %limits.1) | copy-start | bytes 292
  6.9 2.1 %copy-start.3 = (f32[26]{0:T(128)S(1)}, f32[26]{0:T(128)}, u32[]{:S(2)}) copy-start(f32[26]{0:T(128)} %constant.11.clone.rest_2_) | copy-start | bytes 316
  132.2 2.2 %copy-start.4 = (f32[96,45,128]{2,1,0:T(8,128)S(1)}, f32[96,45,128]{2,1,0:T(8,128)}, u32[]{:S(2)}) copy-start(f32[96,45,128]{2,1,0:T(8,128)} %get-tuple-element.6) | copy-start | bytes 6635524

commit v2 on v1

--- a/solution.py
+++ b/solution.py
@@ -31,20 +31,23 @@
 
 def layer_kernel(
     n, lat_dev, own, length, slope, polar, fused,
-    fields, mix, weight, limits, table_f, table_i, *rest,
+    native, mix, weight, limits, table_f, table_i, *rest,
 ):
     if fused:
-        forcing, ocean, cosines, lo, raw, norm = rest[:6]
+        forcing, ocean, cosines, lo_rows, raw, norm = rest[:6]
         rest = rest[6:]
     else:
-        lo = rest[0]
+        lo_rows = rest[0]
         rest = rest[1:]
-    (gathered, wr, wi, arrived, filt, outgoing, tf, ti, force, sums,
+    (fields, staged, lo, gathered, wr, wi, arrived, filt, outgoing, tf, ti,
+     force, sums, squares,
      fwd_send, fwd_recv, ret_send, ret_recv, gat_send, gat_recv,
      local_sem, sum_send, sum_recv) = rest
     rows, pad, channels = fields.shape
     chunks = rows // n
-    per = weight.shape[1]
+    members = rows // lat_dev
+    cells = own * lat_dev
+    per = weight.shape[0]
     modes = per * n
     me = lax.axis_index("lon")
     groups = n // PLANE
@@ -81,14 +84,27 @@
         load.start()
 
     slot = mine * groups + plane
-    gathered[slot, 0:per] = weight[0]
-    gathered[slot, per:2 * per] = weight[1]
-
-    @pl.loop(0, chunks)
-    def _(c):
-        place = pl.multiple_of(me * pad, 16)
-        arrived[c, pl.ds(place, pad)] = fields[c * n + me]
-
+    gathered[slot, 0:per] = weight[:, 0]
+    gathered[slot, per:2 * per] = weight[:, 1]
+    lanes = [slice(part, part + 128) for part in range(0, channels, 128)]
+    for s in range(len(lanes)):
+        staged[s, cells:] = jnp.zeros(((pad - own) * lat_dev, 128), jnp.float32)
+
+    def prepare(m):
+        start = m * cells
+        for s, part in enumerate(lanes):
+            staged[s, 0:cells] = native[start:start + cells, part].astype(jnp.float32)
+
+        @pl.loop(0, lat_dev)
+        def _(j):
+            for s, part in enumerate(lanes):
+                row = staged[s, pl.ds(j, pad, stride=lat_dev), :]
+                fields[m * lat_dev + j, :, part] = row.astype(jnp.bfloat16)
+
+    ready = 0
+    while ready < members and ready * lat_dev < n:
+        prepare(ready)
+        ready += 1
     pl.semaphore_wait(barrier, n - 1)
 
     @pl.loop(1, groups)
@@ -106,6 +122,9 @@
                 fwd_send, fwd_recv.at[c], to,
             ).start()
 
+        place = pl.multiple_of(me * pad, 16)
+        arrived[c, pl.ds(place, pad)] = fields[c * n + me]
+
     scatter(0)
     if groups > 1:
         await_bytes(gathered.at[pl.ds(0, groups - 1)], gat_recv.at[0])
@@ -117,6 +136,9 @@
         send(held, held, gat_send.at[1], gat_recv.at[1], to).start()
 
     for c in range(1, chunks):
+        while ready < members and ready * lat_dev < (c + 1) * n:
+            prepare(ready)
+            ready += 1
         scatter(c)
 
     await_bytes(gathered.at[pl.ds(0, n - groups)], gat_recv.at[1])
@@ -186,31 +208,63 @@
         def _():
             await_bytes(lo.at[r], ret_recv.at[r])
 
+    half = channels // 2
+
+    def keep_row(r, j):
+        for s, part in enumerate(lanes):
+            row = lo[r, :, part].astype(jnp.float32)[0:own]
+            staged[s, pl.ds(j, own, stride=lat_dev), :] = row
+
+    def keep_member(m):
+        start = pl.multiple_of(m * cells, 8)
+        for s, part in enumerate(lanes):
+            lo_rows[pl.ds(start, cells), part] = staged[s, 0:cells].astype(jnp.bfloat16)
+
     if fused:
         loads[2].wait()
-        half = channels // 2
-        sums[me] = jnp.zeros((8, half), jnp.float32)
-
-        def residual(r):
-            j = lax.rem(r, lat_dev)
+        squares[...] = jnp.zeros_like(squares)
+
+        def residual(m, j):
+            r = m * lat_dev + j
             zonal = lo[r, :, 0:half].astype(jnp.float32)
             zonal = (pltpu.roll(zonal, pad - 1, 0) - pltpu.roll(zonal, 1, 0)) * slope
-            north = lo[jnp.minimum(r + 1, rows - 1), :, half:].astype(jnp.float32)
-            south = lo[jnp.maximum(r - 1, 0), :, half:].astype(jnp.float32)
+            north = lo[m * lat_dev + jnp.minimum(j + 1, lat_dev - 1), :, half:].astype(jnp.float32)
+            south = lo[m * lat_dev + jnp.maximum(j - 1, 0), :, half:].astype(jnp.float32)
             merid = (north * cosines[j + 2] - south * cosines[j]) * polar
             flow = (zonal + merid)[0:own]
-            value = ocean[j] * (flow + cosines[j + 1] * force[r])
-            raw[r] = value
-            sums[me, 0:1] += jnp.sum(value * value, axis=0, keepdims=True)
-
-        await_row(0)
-
-        @pl.loop(1, rows)
-        def _(r):
-            await_row(r)
-            residual(r - 1)
-
-        residual(rows - 1)
+            spread = pl.ds(m * cells + j, own, stride=lat_dev)
+            value = flow + cosines[j + 1] * force[spread, :]
+            value = ocean[j].astype(jnp.float32) * value
+            raw[spread, :] = value
+            return value * value
+
+        step = 2 if lat_dev % 2 == 0 else 1
+
+        @pl.loop(0, members)
+        def _(m):
+            await_row(m * lat_dev)
+
+            @pl.loop(0, lat_dev, step=step)
+            def _(j):
+                for k in range(1, step):
+                    await_row(m * lat_dev + j + k)
+
+                @pl.when(j + step < lat_dev)
+                def _():
+                    await_row(m * lat_dev + j + step)
+
+                total = residual(m, j)
+                keep_row(m * lat_dev + j, j)
+                for k in range(1, step):
+                    total += residual(m, j + k)
+                    keep_row(m * lat_dev + j + k, j + k)
+                squares[...] += total
+
+            keep_member(m)
+
+        sums[me] = jnp.broadcast_to(
+            jnp.sum(squares[...], axis=0, keepdims=True) * 0.125, (8, half)
+        )
 
         @pl.loop(1, n)
         def _(i):
@@ -224,9 +278,14 @@
         norm[...] = jnp.broadcast_to(jnp.sqrt(total * scale + 1e-06), (8, half))
         await_bytes(sums.at[pl.ds(0, n - 1)], sum_send)
     else:
-        @pl.loop(0, rows)
-        def _(r):
-            await_row(r)
+        @pl.loop(0, members)
+        def _(m):
+            @pl.loop(0, lat_dev)
+            def _(j):
+                await_row(m * lat_dev + j)
+                keep_row(m * lat_dev + j, j)
+
+            keep_member(m)
 
     await_bytes(fields.at[pl.ds(0, chunks * (n - 1))], fwd_send)
     await_bytes(outgoing.at[pl.ds(0, chunks * (n - 1))], ret_send)
@@ -262,27 +321,33 @@
     forward, inverse = tables(length, modes, n, pad)
     slope = length / (4.0 * math.pi)
     polar = nlat / (2.0 * math.pi)
-    padded = jnp.pad(fields.reshape(rows, own, channels), ((0, 0), (0, pad - own), (0, 0)))
+    cells = own * lat_dev
+
+    def by_longitude(array):
+        return array.transpose(0, 2, 1, 3).reshape(members * cells, array.shape[3])
+
+    def by_latitude(array):
+        shape = (members, own, lat_dev, array.shape[1])
+        return array.reshape(shape).transpose(0, 2, 1, 3)
+
     vmem = pl.BlockSpec(memory_space=pltpu.VMEM)
     smem = pl.BlockSpec(memory_space=pltpu.SMEM)
     away = pl.BlockSpec(memory_space=pl.ANY)
-    operands = [padded, mix_weight, spectral_weight, mode_limit,
+    operands = [by_longitude(fields), mix_weight, spectral_weight.transpose(1, 0, 2), mode_limit,
                 jnp.asarray(forward), jnp.asarray(inverse)]
     in_specs = [vmem, vmem, vmem, smem, away, away]
-    out_shape = [jax.ShapeDtypeStruct((rows, pad, channels), jnp.bfloat16)]
+    out_shape = [jax.ShapeDtypeStruct((members * cells, channels), jnp.bfloat16)]
     if fused:
         latitude = np.float32(-0.5 * math.pi) + (
             np.arange(nlat, dtype=np.float32) + np.float32(0.5)
         ) * np.float32(math.pi / nlat)
         cosines = np.zeros((nlat + 2,), np.float32)
         cosines[1:-1] = np.cos(latitude)
-        ocean = jnp.broadcast_to(
-            land_mask.astype(jnp.float32)[:, :, None], (lat_dev, own, half)
-        )
-        operands += [forcing.reshape(rows, own, half), ocean, jnp.asarray(cosines)]
+        ocean = jnp.broadcast_to(land_mask[:, :, None], (lat_dev, own, half))
+        operands += [by_longitude(forcing), ocean, jnp.asarray(cosines)]
         in_specs += [away, vmem, smem]
         out_shape += [
-            jax.ShapeDtypeStruct((rows, own, half), jnp.float32),
+            jax.ShapeDtypeStruct((members * cells, half), jnp.float32),
             jax.ShapeDtypeStruct((8, half), jnp.float32),
         ]
     gat_rows = -(-2 * per // 8) * 8
@@ -295,6 +360,9 @@
         in_specs=in_specs,
         out_specs=[vmem] * len(out_shape),
         scratch_shapes=[
+            pltpu.VMEM((rows, pad, channels), jnp.bfloat16),
+            pltpu.VMEM((channels // 128, pad * lat_dev, 128), jnp.float32),
+            pltpu.VMEM((rows, pad, channels), jnp.bfloat16),
             pltpu.VMEM((n, gat_rows, channels), jnp.float32),
             pltpu.VMEM((modes, channels), jnp.float32),
             pltpu.VMEM((modes, channels), jnp.float32),
@@ -303,8 +371,9 @@
             pltpu.VMEM((rows, pad, channels), jnp.bfloat16),
             pltpu.VMEM(forward.shape, jnp.bfloat16),
             pltpu.VMEM(inverse.shape, jnp.bfloat16),
-            pltpu.VMEM((rows, own, half) if fused else (8, half), jnp.float32),
+            pltpu.VMEM((members * cells, half) if fused else (8, half), jnp.float32),
             pltpu.VMEM((n, 8, half), jnp.float32),
+            pltpu.VMEM((own, half), jnp.float32),
             dma, dma((chunks,)), dma, dma((rows,)), dma((2,)), dma((2,)),
             dma((3,)), dma, dma,
         ],
@@ -312,9 +381,9 @@
             collective_id=0, has_side_effects=True, vmem_limit_bytes=48 * 2**20
         ),
     )(*operands)
-    layer_out = results[0][:, :own].reshape(fields.shape)
+    layer_out = by_latitude(results[0])
     if fused:
-        residual = results[1].reshape(forcing.shape) / results[2][0]
+        residual = by_latitude(results[1] / results[2][0:1])
         return layer_out, residual
     zonal = extended(layer_out[..., :half], "lon", 2).astype(jnp.float32)
     zonal = (zonal[:, :, 2:] - zonal[:, :, :-2]) * slope

time: 137 us -> 134 us (0.978)
  local copies, waits for them, and re-layouts: 9.82 us -> 6.82 us
    unnamed x16 -> x11, local copies, waits for them, and re-layouts: 8.01 us -> 5.91 us
    pad x1 -> x0, local copies, waits for them, and re-layouts: 1.6 us -> none  [per_device(): jnp.pad(fields.reshape(rows, own, channels), ((0, 0), (0, pad - own), (0,...]
where the time goes in v2:
time: 134 us
  Pallas kernels  123 us (92%)
  local copies, waits for them, and re-layouts  6.82 us (5%)
  other arithmetic  3.13 us (2%)
    pallas_call x1, Pallas kernels, per_device(): pl.pallas_call(functools.partial(layer_kernel, n, lat_dev, own, length, s...  123 us
    unnamed x11, local copies, waits for them, and re-layouts  5.91 us
    div x1, other arithmetic, per_device(): residual = by_latitude(results[1] / results[2][0:1])  3.13 us

profile of v2, /device:TPU:0, one launch (start us, length us, event | category | flops | bytes accessed | tf_op | source)
XLA Modules:
  0.0 133.6 jit_solution(657789192878355502)
XLA Ops:
  0.6 0.9 broadcast_in_dim.2.rest_1_
  1.5 0.0 copy-start
  1.6 1.6 %copy-done = bf16[704,1536]{1,0:T(8,128)(2,1)S(1)} copy-done((bf16[704,1536]{1,0:T(8,128)(2,1)S(1)}, bf16[704,1536]{1,0:T(8,128)(2,1)}, u32[]{:S(2)}) %copy-start) | copy-done | bytes 2162712
  3.2 0.0 copy-start.1
  3.2 0.9 copy-done.1
  4.1 0.0 copy-start.2
  4.1 0.7 copy-done.2
  4.8 0.0 copy-start.3
  4.8 0.7 copy-done.3
  5.5 0.0 copy-start.4
  5.5 0.7 copy-done.4
  6.1 123.0 %shard_map.104 = (bf16[4320,256]{1,0:T(8,128)(2,1)S(1)}, f32[4320,128]{1,0:T(8,128)}, f32[8,128]{1,0:T(8,128)S(1)}) custom-call(bf16[4320,256]{1,0:T(8,128)(2,1)} %bitcast.17, bf16[256,256]{1,0:T(8,128)(2,1)S(1)} %copy-done.1, f32[11,2,256]{2,1,0:T(2,128)S(1)} %bitcast.16, s32[24]{0:T(128)S(1)} %copy-done.3, bf16[704,1536]{1,0:T(8,128)(2,1)S(1)} %copy-done, ...), custom_call_target="tpu_custom_call" | custom-call | tf_op jit(solution)/shard_map/pallas_call | solution.py:355
  129.1 3.1 %broadcast_divide_fusion = f32[4320,128]{1,0:T(8,128)} fusion(f32[4320,128]{1,0:T(8,128)} %get-tuple-element.6, f32[128]{0:T(128)S(1)} %slice_bitcast_fusion), kind=kLoop, calls=%fused_computation | loop fusion | flops 552960 | bytes 4424192 | tf_op jit(solution)/shard_map/div | solution.py:386
  132.3 1.4 %copy.12 = bf16[4,24,45,256]{3,1,2,0:T(8,128)(2,1)} copy(bf16[4,24,45,256]{3,1,2,0:T(8,128)(2,1)S(1)} %bitcast.15) | data formatting | bytes 4423680
  (1 shorter events, 0.0 us)
Async XLA Ops:
  1.5 1.6 %copy-start = (bf16[704,1536]{1,0:T(8,128)(2,1)S(1)}, bf16[704,1536]{1,0:T(8,128)(2,1)}, u32[]{:S(2)}) copy-start(bf16[704,1536]{1,0:T(8,128)(2,1)} %constant.6.clone.table_f) | copy-start | bytes 6488068
  3.2 0.9 copy-start.1
  4.1 0.7 copy-start.2
  4.8 0.7 copy-start.3
  5.5 0.7 copy-start.4

commit v3 on v2

--- a/solution.py
+++ b/solution.py
@@ -31,15 +31,15 @@
 
 def layer_kernel(
     n, lat_dev, own, length, slope, polar, fused,
-    native, mix, weight, limits, table_f, table_i, *rest,
+    fields_in, mix_in, weight_in, limits_in, table_f, table_i, *rest,
 ):
     if fused:
-        forcing, ocean, cosines, lo_rows, raw, norm = rest[:6]
-        rest = rest[6:]
+        forcing, mask_in, cos_in, lo_rows, raw = rest[:5]
+        rest = rest[5:]
     else:
         lo_rows = rest[0]
         rest = rest[1:]
-    (fields, staged, lo, gathered, wr, wi, arrived, filt, outgoing, tf, ti,
+    (native, mix, weight, limits, mask, cosines, ocean, fields, staged, lo, gathered, wr, wi, arrived, filt, outgoing, tf, ti,
      force, sums, squares,
      fwd_send, fwd_recv, ret_send, ret_recv, gat_send, gat_recv,
      local_sem, sum_send, sum_recv) = rest
@@ -74,14 +74,18 @@
             barrier, inc=1, device_id={"lon": lax.rem(me + i, n)}, device_id_type=MESH
         )
 
+    pairs = [(weight_in, weight)]
+    for m in range(members):
+        pairs.append((fields_in.at[m], native.at[m]))
+    pairs += [(table_f, tf), (table_i, ti), (mix_in, mix), (limits_in, limits)]
+    if fused:
+        pairs += [(mask_in, mask), (cos_in, cosines), (forcing, force)]
     loads = [
-        pltpu.make_async_copy(table_f, tf, local_sem.at[0]),
-        pltpu.make_async_copy(table_i, ti, local_sem.at[1]),
+        pltpu.make_async_copy(src, dst, local_sem.at[i]) for i, (src, dst) in enumerate(pairs)
     ]
-    if fused:
-        loads.append(pltpu.make_async_copy(forcing, force, local_sem.at[2]))
     for load in loads:
         load.start()
+    loads[0].wait()
 
     slot = mine * groups + plane
     gathered[slot, 0:per] = weight[:, 0]
@@ -91,9 +95,9 @@
         staged[s, cells:] = jnp.zeros(((pad - own) * lat_dev, 128), jnp.float32)
 
     def prepare(m):
-        start = m * cells
+        loads[1 + m].wait()
         for s, part in enumerate(lanes):
-            staged[s, 0:cells] = native[start:start + cells, part].astype(jnp.float32)
+            staged[s, 0:cells] = native[m, :, part].astype(jnp.float32)
 
         @pl.loop(0, lat_dev)
         def _(j):
@@ -119,7 +123,7 @@
             place = pl.multiple_of(me * pad, 16)
             send(
                 fields.at[c * n + to], arrived.at[c, pl.ds(place, pad)],
-                fwd_send, fwd_recv.at[c], to,
+                fwd_send.at[c], fwd_recv.at[c], to,
             ).start()
 
         place = pl.multiple_of(me * pad, 16)
@@ -139,15 +143,31 @@
         while ready < members and ready * lat_dev < (c + 1) * n:
             prepare(ready)
             ready += 1
+        if c >= 2:
+            await_bytes(fields.at[pl.ds(0, n - 1)], fwd_send.at[c - 2])
         scatter(c)
+
+    for load in loads[1 + members:]:
+        load.wait()
+    if fused:
+        eye = [lax.broadcasted_iota(jnp.int32, (own, own), k) for k in range(2)]
+        eye = (eye[0] == eye[1]).astype(jnp.bfloat16)
+        turned = lax.dot_general(
+            eye, mask[...].astype(jnp.float32).astype(jnp.bfloat16), (((1,), (1,)), ((), ())),
+            preferred_element_type=jnp.float32,
+        ).astype(jnp.bfloat16)
+        row_of = lax.broadcasted_iota(jnp.int32, (lat_dev, channels // 2), 0)
+
+        @pl.loop(0, lat_dev)
+        def _(j):
+            chosen = (row_of == j).astype(jnp.float32).astype(jnp.bfloat16)
+            ocean[j] = jnp.dot(turned, chosen, preferred_element_type=jnp.float32)
 
     await_bytes(gathered.at[pl.ds(0, n - groups)], gat_recv.at[1])
     for device in range(n):
         place = (device % PLANE) * groups + device // PLANE
         wr[device * per:(device + 1) * per] = gathered[place, 0:per]
         wi[device * per:(device + 1) * per] = gathered[place, per:2 * per]
-    loads[0].wait()
-    loads[1].wait()
 
     @pl.loop(0, chunks)
     def _(c):
@@ -221,7 +241,6 @@
             lo_rows[pl.ds(start, cells), part] = staged[s, 0:cells].astype(jnp.bfloat16)
 
     if fused:
-        loads[2].wait()
         squares[...] = jnp.zeros_like(squares)
 
         def residual(m, j):
@@ -230,11 +249,11 @@
             zonal = (pltpu.roll(zonal, pad - 1, 0) - pltpu.roll(zonal, 1, 0)) * slope
             north = lo[m * lat_dev + jnp.minimum(j + 1, lat_dev - 1), :, half:].astype(jnp.float32)
             south = lo[m * lat_dev + jnp.maximum(j - 1, 0), :, half:].astype(jnp.float32)
-            merid = (north * cosines[j + 2] - south * cosines[j]) * polar
+            merid = (north * cosines[pl.ds(j + 2, 1)] - south * cosines[pl.ds(j, 1)]) * polar
             flow = (zonal + merid)[0:own]
             spread = pl.ds(m * cells + j, own, stride=lat_dev)
-            value = flow + cosines[j + 1] * force[spread, :]
-            value = ocean[j].astype(jnp.float32) * value
+            value = flow + cosines[pl.ds(j + 1, 1)] * force[spread, :]
+            value = ocean[j] * value
             raw[spread, :] = value
             return value * value
 
@@ -275,7 +294,15 @@
         total = jnp.sum(sums[...], axis=0)
         total = jnp.sum(jnp.sum(total, axis=0, keepdims=True), axis=1, keepdims=True)
         scale = 1.0 / (rows * own * n * half)
-        norm[...] = jnp.broadcast_to(jnp.sqrt(total * scale + 1e-06), (8, half))
+        inverse = 1.0 / jnp.sqrt(total * scale + 1e-06)
+
+        step = lat_dev * own // 5
+
+        @pl.loop(0, 5 * members)
+        def _(r):
+            part = pl.ds(pl.multiple_of(r * step, 8), step)
+            raw[part] = raw[part] * inverse
+
         await_bytes(sums.at[pl.ds(0, n - 1)], sum_send)
     else:
         @pl.loop(0, members)
@@ -287,7 +314,8 @@
 
             keep_member(m)
 
-    await_bytes(fields.at[pl.ds(0, chunks * (n - 1))], fwd_send)
+    for c in range(max(chunks - 2, 0), chunks):
+        await_bytes(fields.at[pl.ds(0, n - 1)], fwd_send.at[c])
     await_bytes(outgoing.at[pl.ds(0, chunks * (n - 1))], ret_send)
     if groups > 1:
         await_bytes(gathered.at[pl.ds(0, groups - 1)], gat_send.at[0])
@@ -331,24 +359,21 @@
         return array.reshape(shape).transpose(0, 2, 1, 3)
 
     vmem = pl.BlockSpec(memory_space=pltpu.VMEM)
-    smem = pl.BlockSpec(memory_space=pltpu.SMEM)
-    away = pl.BlockSpec(memory_space=pl.ANY)
-    operands = [by_longitude(fields), mix_weight, spectral_weight.transpose(1, 0, 2), mode_limit,
+    away = pl.BlockSpec(memory_space=pltpu.HBM)
+    operands = [by_longitude(fields).reshape(members, cells, channels), mix_weight, spectral_weight.transpose(1, 0, 2), mode_limit,
                 jnp.asarray(forward), jnp.asarray(inverse)]
-    in_specs = [vmem, vmem, vmem, smem, away, away]
+    in_specs = [away] * 6
     out_shape = [jax.ShapeDtypeStruct((members * cells, channels), jnp.bfloat16)]
     if fused:
         latitude = np.float32(-0.5 * math.pi) + (
             np.arange(nlat, dtype=np.float32) + np.float32(0.5)
         ) * np.float32(math.pi / nlat)
-        cosines = np.zeros((nlat + 2,), np.float32)
-        cosines[1:-1] = np.cos(latitude)
-        ocean = jnp.broadcast_to(land_mask[:, :, None], (lat_dev, own, half))
-        operands += [by_longitude(forcing), ocean, jnp.asarray(cosines)]
-        in_specs += [away, vmem, smem]
+        cosines = np.zeros((nlat + 2, half), np.float32)
+        cosines[1:-1] = np.cos(latitude)[:, None]
+        operands += [by_longitude(forcing), land_mask, jnp.asarray(cosines)]
+        in_specs += [away] * 3
         out_shape += [
             jax.ShapeDtypeStruct((members * cells, half), jnp.float32),
-            jax.ShapeDtypeStruct((8, half), jnp.float32),
         ]
     gat_rows = -(-2 * per // 8) * 8
     dma = pltpu.SemaphoreType.DMA
@@ -360,6 +385,13 @@
         in_specs=in_specs,
         out_specs=[vmem] * len(out_shape),
         scratch_shapes=[
+            pltpu.VMEM((members, cells, channels), jnp.bfloat16),
+            pltpu.VMEM(mix_weight.shape, jnp.bfloat16),
+            pltpu.VMEM((per, 2, channels), jnp.float32),
+            pltpu.SMEM(mode_limit.shape, jnp.int32),
+            pltpu.VMEM(land_mask.shape, jnp.int32),
+            pltpu.VMEM((nlat + 2, half), jnp.float32),
+            pltpu.VMEM((lat_dev, own, half), jnp.float32),
             pltpu.VMEM((rows, pad, channels), jnp.bfloat16),
             pltpu.VMEM((channels // 128, pad * lat_dev, 128), jnp.float32),
             pltpu.VMEM((rows, pad, channels), jnp.bfloat16),
@@ -374,16 +406,16 @@
             pltpu.VMEM((members * cells, half) if fused else (8, half), jnp.float32),
             pltpu.VMEM((n, 8, half), jnp.float32),
             pltpu.VMEM((own, half), jnp.float32),
-            dma, dma((chunks,)), dma, dma((rows,)), dma((2,)), dma((2,)),
-            dma((3,)), dma, dma,
+            dma((chunks,)), dma((chunks,)), dma, dma((rows,)), dma((2,)), dma((2,)),
+            dma((members + 8,)), dma, dma,
         ],
         compiler_params=pltpu.CompilerParams(
-            collective_id=0, has_side_effects=True, vmem_limit_bytes=48 * 2**20
+            collective_id=0, has_side_effects=True, vmem_limit_bytes=40 * 2**20
         ),
     )(*operands)
     layer_out = by_latitude(results[0])
     if fused:
-        residual = by_latitude(results[1] / results[2][0:1])
+        residual = by_latitude(results[1])
         return layer_out, residual
     zonal = extended(layer_out[..., :half], "lon", 2).astype(jnp.float32)
     zonal = (zonal[:, :, 2:] - zonal[:, :, :-2]) * slope

time: 134 us -> 134 us (level)
  local copies, waits for them, and re-layouts: 6.82 us -> 12.9 us
  other arithmetic: 3.13 us -> 0 us
  Pallas kernels: 123 us -> 120 us
    unnamed x11 -> x20, local copies, waits for them, and re-layouts: 5.91 us -> 12.9 us
    pallas_call x1, Pallas kernels: 123 us -> 120 us  [per_device(): pl.pallas_call(functools.partial(layer_kernel, n, lat_dev, own, length, s...]
    div x1 -> x0, other arithmetic: 3.13 us -> none  [per_device(): residual = by_latitude(results[1] / results[2][0:1])]
where the time goes in v3:
time: 134 us; the launch traced here: 133 us
  Pallas kernels  120 us (90%)
  local copies, waits for them, and re-layouts  12.9 us (10%)
    pallas_call x1, Pallas kernels, per_device(): pl.pallas_call(functools.partial(layer_kernel, n, lat_dev, own, length, s...  120 us
    unnamed x20, local copies, waits for them, and re-layouts  12.9 us

profile of v3, /device:TPU:0, one launch (start us, length us, event | category | flops | bytes accessed | tf_op | source)
XLA Modules:
  0.0 133.1 jit_solution(14919022668511756357)
XLA Ops:
  0.6 0.0 copy-start
  0.6 1.7 %copy-done = bf16[1536,704]{1,0:T(8,128)(2,1)S(1)} copy-done((bf16[1536,704]{1,0:T(8,128)(2,1)S(1)}, bf16[1536,704]{1,0:T(8,128)(2,1)}, u32[]{:S(2)}) %copy-start) | copy-done | bytes 2162712
  2.3 0.0 copy-start.1
  2.3 1.6 %copy-done.1 = bf16[4,24,45,256]{3,1,2,0:T(8,128)(2,1)S(1)} copy-done((bf16[4,24,45,256]{3,1,2,0:T(8,128)(2,1)S(1)}, bf16[4,24,45,256]{3,1,2,0:T(8,128)(2,1)}, u32[]{:S(2)}) %copy-start.1) | copy-done | bytes 2211864
  3.9 0.0 copy-start.2
  3.9 1.6 %copy-done.2 = f32[4,24,45,128]{3,1,2,0:T(8,128)S(1)} copy-done((f32[4,24,45,128]{3,1,2,0:T(8,128)S(1)}, f32[4,24,45,128]{3,1,2,0:T(8,128)}, u32[]{:S(2)}) %copy-start.2) | copy-done | bytes 2211864
  5.5 0.0 copy-start.3
  5.6 1.6 %copy-done.3 = bf16[704,1536]{1,0:T(8,128)(2,1)S(1)} copy-done((bf16[704,1536]{1,0:T(8,128)(2,1)S(1)}, bf16[704,1536]{1,0:T(8,128)(2,1)}, u32[]{:S(2)}) %copy-start.3) | copy-done | bytes 2162712
  7.2 0.0 copy-start.4
  7.2 0.9 copy-done.4
  8.1 0.0 copy-start.5
  8.1 0.7 copy-done.5
  8.8 0.0 copy-start.6
  8.8 0.7 copy-done.6
  9.5 0.0 copy-start.7
  9.5 0.7 copy-done.7
  10.2 0.0 copy-start.8
  10.2 0.7 copy-done.8
  10.9 119.5 %shard_map.104 = (bf16[4320,256]{1,0:T(8,128)(2,1)S(1)}, f32[4320,128]{1,0:T(8,128)S(1)}) custom-call(bf16[4,1080,256]{2,1,0:T(8,128)(2,1)S(1)} %bitcast.13, bf16[256,256]{1,0:T(8,128)(2,1)S(1)} %copy-done.4, f32[11,2,256]{2,1,0:T(2,128)S(1)} %bitcast.17, s32[24]{0:T(128)S(1)} %copy-done.8, bf16[704,1536]{1,0:T(8,128)(2,1)S(1)} %copy-done.3, ...), custom_call_target="tpu_custom_call" | custom-call | tf_op jit(solution)/shard_map/pallas_call | solution.py:380
  130.4 1.4 %copy.13 = bf16[4,24,45,256]{3,1,2,0:T(8,128)(2,1)} copy(bf16[4,24,45,256]{3,1,2,0:T(8,128)(2,1)S(1)} %bitcast.16) | data formatting | bytes 4423680
  131.8 1.4 %copy.14 = f32[4,24,45,128]{3,1,2,0:T(8,128)} copy(f32[4,24,45,128]{3,1,2,0:T(8,128)S(1)} %bitcast.15) | data formatting | bytes 4423680
Async XLA Ops:
  0.6 1.7 %copy-start = (bf16[1536,704]{1,0:T(8,128)(2,1)S(1)}, bf16[1536,704]{1,0:T(8,128)(2,1)}, u32[]{:S(2)}) copy-start(bf16[1536,704]{1,0:T(8,128)(2,1)} %constant.7.clone.table_i) | copy-start | bytes 6488068
  2.3 1.6 %copy-start.1 = (bf16[4,24,45,256]{3,1,2,0:T(8,128)(2,1)S(1)}, bf16[4,24,45,256]{3,1,2,0:T(8,128)(2,1)}, u32[]{:S(2)}) copy-start(bf16[4,24,45,256]{3,1,2,0:T(8,128)(2,1)} %param.9) | copy-start | bytes 6635524
  3.9 1.6 %copy-start.2 = (f32[4,24,45,128]{3,1,2,0:T(8,128)S(1)}, f32[4,24,45,128]{3,1,2,0:T(8,128)}, u32[]{:S(2)}) copy-start(f32[4,24,45,128]{3,1,2,0:T(8,128)} %param.14) | copy-start | bytes 6635524
  5.5 1.6 %copy-start.3 = (bf16[704,1536]{1,0:T(8,128)(2,1)S(1)}, bf16[704,1536]{1,0:T(8,128)(2,1)}, u32[]{:S(2)}) copy-start(bf16[704,1536]{1,0:T(8,128)(2,1)} %constant.6.clone.table_f) | copy-start | bytes 6488068
  7.2 0.9 copy-start.4
  8.1 0.7 copy-start.5
  8.8 0.7 copy-start.6
  9.5 0.7 copy-start.7
  10.2 0.7 copy-start.8

commit v4 on v3

--- a/solution.py
+++ b/solution.py
@@ -410,7 +410,7 @@
             dma((members + 8,)), dma, dma,
         ],
         compiler_params=pltpu.CompilerParams(
-            collective_id=0, has_side_effects=True, vmem_limit_bytes=40 * 2**20
+            collective_id=0, has_side_effects=True, vmem_limit_bytes=62 * 2**20
         ),
     )(*operands)
     layer_out = by_latitude(results[0])

time: 134 us -> 127 us (0.948)
  local copies, waits for them, and re-layouts: 12.9 us -> 4.63 us
  Pallas kernels: 120 us -> 122 us
    unnamed x20 -> x4, local copies, waits for them, and re-layouts: 12.9 us -> 4.63 us
    pallas_call x1, Pallas kernels: 120 us -> 122 us  [per_device(): pl.pallas_call(functools.partial(layer_kernel, n, lat_dev, own, length, s...]
where the time goes in v4:
time: 127 us
  Pallas kernels  122 us (96%)
  local copies, waits for them, and re-layouts  4.63 us (4%)
    pallas_call x1, Pallas kernels, per_device(): pl.pallas_call(functools.partial(layer_kernel, n, lat_dev, own, length, s...  122 us
    unnamed x4, local copies, waits for them, and re-layouts  4.63 us

profile of v4, /device:TPU:0, one launch (start us, length us, event | category | flops | bytes accessed | tf_op | source)
XLA Modules:
  0.0 127.0 jit_solution(2569204840493552302)
XLA Ops:
  0.6 121.8 %shard_map.104 = (bf16[4320,256]{1,0:T(8,128)(2,1)}, f32[4320,128]{1,0:T(8,128)}) custom-call(bf16[4,1080,256]{2,1,0:T(8,128)(2,1)} %bitcast.13, bf16[256,256]{1,0:T(8,128)(2,1)} %mix_in.1, f32[11,2,256]{2,1,0:T(2,128)} %bitcast.17, s32[24]{0:T(128)} %limits_in.1, bf16[704,1536]{1,0:T(8,128)(2,1)} %constant.6.clone.table_f, ...), custom_call_target="tpu_custom_call" | custom-call | tf_op jit(solution)/shard_map/pallas_call | solution.py:380
  122.4 0.0 copy-start
  122.4 3.3 %copy.13 = bf16[4,24,45,256]{3,1,2,0:T(8,128)(2,1)} copy(bf16[4,24,45,256]{3,1,2,0:T(8,128)(2,1)} %bitcast.16) | data formatting | bytes 4423680
  125.7 0.0 copy-done
  125.7 1.4 %copy.14 = f32[4,24,45,128]{3,1,2,0:T(8,128)} copy(f32[4,24,45,128]{3,1,2,0:T(8,128)S(1)} %bitcast.15) | data formatting | bytes 4423680
Async XLA Ops:
  122.4 3.3 %copy-start = (f32[4320,128]{1,0:T(8,128)S(1)}, f32[4320,128]{1,0:T(8,128)}, u32[]{:S(2)}) copy-start(f32[4320,128]{1,0:T(8,128)} %get-tuple-element.5) | copy-start | bytes 6635524

commit v5 on v4

--- a/solution.py
+++ b/solution.py
@@ -39,7 +39,7 @@
     else:
         lo_rows = rest[0]
         rest = rest[1:]
-    (native, mix, weight, limits, mask, cosines, ocean, fields, staged, lo, gathered, wr, wi, arrived, filt, outgoing, tf, ti,
+    (kept, out_sem, native, mix, weight, limits, mask, cosines, ocean, fields, staged, lo, gathered, wr, wi, arrived, filt, outgoing, tf, ti,
      force, sums, squares,
      fwd_send, fwd_recv, ret_send, ret_recv, gat_send, gat_recv,
      local_sem, sum_send, sum_recv) = rest
@@ -83,7 +83,7 @@
     loads = [
         pltpu.make_async_copy(src, dst, local_sem.at[i]) for i, (src, dst) in enumerate(pairs)
     ]
-    for load in loads:
+    for load in loads[:1 + members]:
         load.start()
     loads[0].wait()
 
@@ -130,6 +130,8 @@
         arrived[c, pl.ds(place, pad)] = fields[c * n + me]
 
     scatter(0)
+    for load in loads[1 + members:]:
+        load.start()
     if groups > 1:
         await_bytes(gathered.at[pl.ds(0, groups - 1)], gat_recv.at[0])
     held = gathered.at[pl.ds(mine * groups, groups)]
@@ -236,9 +238,9 @@
             staged[s, pl.ds(j, own, stride=lat_dev), :] = row
 
     def keep_member(m):
-        start = pl.multiple_of(m * cells, 8)
         for s, part in enumerate(lanes):
-            lo_rows[pl.ds(start, cells), part] = staged[s, 0:cells].astype(jnp.bfloat16)
+            kept[m, :, part] = staged[s, 0:cells].astype(jnp.bfloat16)
+        pltpu.make_async_copy(kept.at[m], lo_rows.at[m], out_sem.at[m]).start()
 
     if fused:
         squares[...] = jnp.zeros_like(squares)
@@ -314,6 +316,8 @@
 
             keep_member(m)
 
+    for m in range(members):
+        pltpu.make_async_copy(kept.at[m], lo_rows.at[m], out_sem.at[m]).wait()
     for c in range(max(chunks - 2, 0), chunks):
         await_bytes(fields.at[pl.ds(0, n - 1)], fwd_send.at[c])
     await_bytes(outgoing.at[pl.ds(0, chunks * (n - 1))], ret_send)
@@ -355,7 +359,7 @@
         return array.transpose(0, 2, 1, 3).reshape(members * cells, array.shape[3])
 
     def by_latitude(array):
-        shape = (members, own, lat_dev, array.shape[1])
+        shape = (members, own, lat_dev, array.shape[-1])
         return array.reshape(shape).transpose(0, 2, 1, 3)
 
     vmem = pl.BlockSpec(memory_space=pltpu.VMEM)
@@ -363,7 +367,7 @@
     operands = [by_longitude(fields).reshape(members, cells, channels), mix_weight, spectral_weight.transpose(1, 0, 2), mode_limit,
                 jnp.asarray(forward), jnp.asarray(inverse)]
     in_specs = [away] * 6
-    out_shape = [jax.ShapeDtypeStruct((members * cells, channels), jnp.bfloat16)]
+    out_shape = [jax.ShapeDtypeStruct((members, cells, channels), jnp.bfloat16)]
     if fused:
         latitude = np.float32(-0.5 * math.pi) + (
             np.arange(nlat, dtype=np.float32) + np.float32(0.5)
@@ -383,8 +387,10 @@
         ),
         out_shape=out_shape,
         in_specs=in_specs,
-        out_specs=[vmem] * len(out_shape),
+        out_specs=[away] + [vmem] * (len(out_shape) - 1),
         scratch_shapes=[
+            pltpu.VMEM((members, cells, channels), jnp.bfloat16),
+            dma((members,)),
             pltpu.VMEM((members, cells, channels), jnp.bfloat16),
             pltpu.VMEM(mix_weight.shape, jnp.bfloat16),
             pltpu.VMEM((per, 2, channels), jnp.float32),

time: 127 us -> 127 us (level)
  no operation moved by 1% of the time
where the time goes in v5:
time: 127 us; the launch traced here: 126 us
  Pallas kernels  121 us (95%)
  local copies, waits for them, and re-layouts  4.63 us (4%)
    pallas_call x1, Pallas kernels, per_device(): pl.pallas_call(functools.partial(layer_kernel, n, lat_dev, own, length, s...  121 us
    unnamed x4, local copies, waits for them, and re-layouts  4.63 us

profile of v5, /device:TPU:0, one launch (start us, length us, event | category | flops | bytes accessed | tf_op | source)
XLA Modules:
  0.0 126.4 jit_solution(4133579806906146324)
XLA Ops:
  0.6 121.1 %shard_map.104 = (bf16[4,1080,256]{2,1,0:T(8,128)(2,1)}, f32[4320,128]{1,0:T(8,128)}) custom-call(bf16[4,1080,256]{2,1,0:T(8,128)(2,1)} %bitcast.13, bf16[256,256]{1,0:T(8,128)(2,1)} %mix_in.1, f32[11,2,256]{2,1,0:T(2,128)} %bitcast.17, s32[24]{0:T(128)} %limits_in.1, bf16[704,1536]{1,0:T(8,128)(2,1)} %constant.6.clone.table_f, ...), custom_call_target="tpu_custom_call" | custom-call | tf_op jit(solution)/shard_map/pallas_call | solution.py:384
  121.8 0.0 copy-start
  121.8 3.3 %copy.13 = bf16[4,24,45,256]{3,1,2,0:T(8,128)(2,1)} copy(bf16[4,24,45,256]{3,1,2,0:T(8,128)(2,1)} %bitcast.16) | data formatting | bytes 4423680
  125.0 0.0 copy-done
  125.0 1.4 %copy.14 = f32[4,24,45,128]{3,1,2,0:T(8,128)} copy(f32[4,24,45,128]{3,1,2,0:T(8,128)S(1)} %bitcast.15) | data formatting | bytes 4423680
Async XLA Ops:
  121.8 3.3 %copy-start = (f32[4320,128]{1,0:T(8,128)S(1)}, f32[4320,128]{1,0:T(8,128)}, u32[]{:S(2)}) copy-start(f32[4320,128]{1,0:T(8,128)} %get-tuple-element.5) | copy-start | bytes 6635524
